TPU v7x, 32 devices: a whole 2x2x4 slice. The times are simulated.
32 devices in a mesh: dp: 4 (over z), ctx: 8 (over y, x, core).
Axes of the slice: x: 2, y: 2, z: 4, core: 2. Of those that a mesh axis runs over, the one named last changes fastest.
Arguments:
- hidden_in: bfloat16 [4, 1024, 768], P('dp', 'ctx'), may hold values from -6 to 6
- segment_ids: int32 [4, 1024], P('dp', 'ctx'), may hold values from 0 to 4, as said below
- w_qkv: bfloat16 [768, 2304], P('dp'), may hold values from -0.21875 to 0.21875
- w_out: bfloat16 [768, 768], P('dp'), may hold values from -4 to 4
- w_in: bfloat16 [768, 2304], P('dp'), may hold values from -0.21875 to 0.21875
- w_down: bfloat16 [1152, 768], P('dp'), may hold values from -0.1875 to 0.1875
- gain_attn: bfloat16 [768], P('dp'), may hold values from 0.5 to 1.5
- gain_mlp: bfloat16 [768], P('dp'), may hold values from 0.5 to 1.5
- cotangent: bfloat16 [4, 1024, 768], P('dp', 'ctx'), may hold values from -6 to 6
Outputs:
- output: bfloat16 [4, 1024, 768], P('dp', 'ctx')
- grad_input: float32 [4, 1024, 768], P('dp', 'ctx')
- grad_qkv: float32 [768, 2304], P('dp')
- grad_out: float32 [768, 768], P('dp')
- grad_in: float32 [768, 2304], P('dp')
- grad_down: float32 [1152, 768], P('dp')
- grad_gain_attn: float32 [768], P('dp')
- grad_gain_mlp: float32 [768], P('dp')
Inputs may be any that keep to these rules, and one draw needn't show every extreme that they name: `segment_ids`: ids never fall along a sequence; each sequence holds documents 0 to 4; document 2 begins within the first 128 tokens and ends within the last 128; every other document is shorter than 128 tokens.
All inputs are finite; a program needn't handle non-finite values.
Results may differ from a plain program's by a relative error of at most 0.024.
Values may be sent and summed in bfloat16 or wider, within the bound.
A program may use at most 256 MiB of HBM per device.

v0:
```python
import jax
import jax.numpy as jnp
from jax import lax
from jax.sharding import PartitionSpec as P

HEADS = 12
EPSILON = 1e-05
ROPE_THETA = 160000.0
NEGATIVE = -1e30


def layer_norm(values, gain_row):
    average = jnp.mean(values, axis=-1, keepdims=True)
    centred = values - average
    spread = jnp.mean(centred * centred, axis=-1, keepdims=True)
    return centred * lax.rsqrt(spread + EPSILON) * gain_row


def rope_tables(first_row, row_count, head_size):
    position = (first_row + jnp.arange(row_count, dtype=jnp.int32)).astype(jnp.float32)
    frequency = ROPE_THETA ** (-jnp.arange(0, head_size, 2, dtype=jnp.float32) / head_size)
    angles = position[:, None] * frequency[None, :]
    angles = jnp.concatenate([angles, angles], axis=-1)
    return (jnp.cos(angles)[:, None, :], jnp.sin(angles)[:, None, :])


def rotary(values, cosines, sines):
    half_size = values.shape[-1] // 2
    turned = jnp.concatenate([-values[..., half_size:], values[..., :half_size]], axis=-1)
    return values * cosines + turned * sines


def rotary_back(grads, cosines, sines):
    half_size = grads.shape[-1] // 2
    shifted = grads * sines
    return grads * cosines + jnp.concatenate(
        [shifted[..., half_size:], -shifted[..., :half_size]], axis=-1
    )


def geglu(gate_in, gate_up):
    return jax.nn.gelu(gate_in, approximate=False) * gate_up


def contract_rows(left_side, right_side):
    return lax.dot_general(
        left_side, right_side, (((0,), (0,)), ((), ())), preferred_element_type=jnp.float32
    )


def contract_cols(left_side, right_side):
    return lax.dot_general(
        left_side, right_side, (((1,), (1,)), ((), ())), preferred_element_type=jnp.float32
    )


def local(hidden_in, segment_ids, w_qkv, w_out, w_in, w_down, gain_attn, gain_mlp, cotangent):
    local_rows = hidden_in.shape[1]
    model_width = hidden_in.shape[2]
    head_count = HEADS
    head_size = model_width // head_count
    score_scale = head_size ** (-0.5)
    head_shape = (local_rows, head_count, head_size)
    shards = (w_qkv, w_out, w_in, w_down, gain_attn, gain_mlp)
    qkv_full, out_full, in_full, down_full, attn_scale, mlp_scale = (
        lax.all_gather(shards[0], "dp", axis=0, tiled=True),
        lax.all_gather(shards[1], "dp", axis=0, tiled=True),
        lax.all_gather(shards[2], "dp", axis=0, tiled=True),
        lax.all_gather(shards[3], "dp", axis=0, tiled=True),
        lax.all_gather(shards[4], "dp", axis=0, tiled=True),
        lax.all_gather(shards[5], "dp", axis=0, tiled=True),
    )
    hidden_units = in_full.shape[1] // 2
    source = hidden_in[0].astype(jnp.float32)
    own_ids = segment_ids[0]
    cosines, sines = rope_tables(lax.axis_index("ctx") * local_rows, local_rows, head_size)
    normed_one = layer_norm(source, attn_scale.astype(jnp.float32)).astype(jnp.bfloat16)
    projected = jnp.dot(normed_one, qkv_full, preferred_element_type=jnp.float32)
    queries = rotary(projected[:, :model_width].reshape(head_shape), cosines, sines).astype(
        jnp.bfloat16
    )
    own_keys = rotary(
        projected[:, model_width : 2 * model_width].reshape(head_shape), cosines, sines
    ).astype(jnp.bfloat16)
    value_flat = projected[:, 2 * model_width :].astype(jnp.bfloat16)
    own_values = value_flat.reshape(head_shape)
    key_flat = own_keys.reshape(local_rows, model_width)
    query_flat = queries.reshape(local_rows, model_width)
    highest = jnp.full((head_count, local_rows), NEGATIVE, jnp.float32)
    block_keys = lax.all_gather(key_flat, "ctx", axis=0, tiled=True)
    block_values = lax.all_gather(value_flat, "ctx", axis=0, tiled=True)
    block_ids = lax.all_gather(own_ids, "ctx", axis=0, tiled=True)
    piece_rows = block_keys.shape[0]
    scores = (
        jnp.einsum(
            "qhe,khe->hqk",
            queries,
            block_keys.reshape(piece_rows, head_count, head_size),
            preferred_element_type=jnp.float32,
        )
        * score_scale
    )
    allowed = (own_ids[:, None] == block_ids[None, :])[None]
    scores = jnp.where(allowed, scores, NEGATIVE)
    raised = jnp.maximum(highest, jnp.max(scores, axis=-1))
    weights = jnp.where(allowed, jnp.exp(scores - raised[..., None]), 0.0)
    row_total = jnp.sum(weights, axis=-1)
    update = jnp.einsum(
        "hqk,khe->qhe",
        weights.astype(jnp.bfloat16),
        block_values.reshape(piece_rows, head_count, head_size),
        preferred_element_type=jnp.float32,
    )
    summed = update
    highest, row_total, summed = (raised, row_total, summed)
    attention = summed / jnp.transpose(row_total)[:, :, None]
    log_total = highest + jnp.log(row_total)
    attended = attention.reshape(local_rows, model_width).astype(jnp.bfloat16)
    middle = source + jnp.dot(attended, out_full, preferred_element_type=jnp.float32)
    normed_two = layer_norm(middle, mlp_scale.astype(jnp.float32)).astype(jnp.bfloat16)
    lifted = jnp.dot(normed_two, in_full, preferred_element_type=jnp.float32)
    gate_in = lifted[:, :hidden_units]
    gate_up = lifted[:, hidden_units:]
    mixed_units = geglu(gate_in, gate_up).astype(jnp.bfloat16)
    result = (middle + jnp.dot(mixed_units, down_full, preferred_element_type=jnp.float32)).astype(
        jnp.bfloat16
    )
    qkv_back, out_back, in_back, down_back, attn_back, mlp_back = (
        lax.all_gather(shards[0], "dp", axis=0, tiled=True),
        lax.all_gather(shards[1], "dp", axis=0, tiled=True),
        lax.all_gather(shards[2], "dp", axis=0, tiled=True),
        lax.all_gather(shards[3], "dp", axis=0, tiled=True),
        lax.all_gather(shards[4], "dp", axis=0, tiled=True),
        lax.all_gather(shards[5], "dp", axis=0, tiled=True),
    )
    upstream = cotangent[0]
    grad_down = contract_rows(mixed_units, upstream)
    grad_mixed = contract_cols(upstream, down_back)
    _, pull_gate = jax.vjp(geglu, gate_in, gate_up)
    grad_gate_in, grad_gate_up = pull_gate(grad_mixed)
    grad_lifted = jnp.concatenate([grad_gate_in, grad_gate_up], axis=1).astype(jnp.bfloat16)
    grad_in = contract_rows(normed_two, grad_lifted)
    grad_normed_two = contract_cols(grad_lifted, in_back)
    _, pull_two = jax.vjp(layer_norm, middle, mlp_back.astype(jnp.float32))
    grad_middle_part, grad_mlp_gain = pull_two(grad_normed_two)
    grad_middle = upstream.astype(jnp.float32) + grad_middle_part
    grad_branch = grad_middle.astype(jnp.bfloat16)
    grad_out = contract_rows(attended, grad_branch)
    grad_attended = contract_cols(grad_branch, out_back).astype(jnp.bfloat16)
    grad_heads = grad_attended.reshape(head_shape)
    products = jnp.transpose(jnp.sum(grad_heads.astype(jnp.float32) * attention, axis=-1))
    all_log, all_products, all_ids = (
        lax.all_gather(log_total, "ctx", axis=1, tiled=True),
        lax.all_gather(products, "ctx", axis=1, tiled=True),
        lax.all_gather(own_ids, "ctx", axis=0, tiled=True),
    )
    block_keys = lax.all_gather(key_flat, "ctx", axis=0, tiled=True)
    block_values = lax.all_gather(value_flat, "ctx", axis=0, tiled=True)
    block_ids = lax.all_gather(own_ids, "ctx", axis=0, tiled=True)
    piece_rows = block_keys.shape[0]
    key_heads = block_keys.reshape(piece_rows, head_count, head_size)
    scores = (
        jnp.einsum("qhe,khe->hqk", queries, key_heads, preferred_element_type=jnp.float32)
        * score_scale
    )
    allowed = (own_ids[:, None] == block_ids[None, :])[None]
    probabilities = jnp.where(allowed, jnp.exp(scores - log_total[..., None]), 0.0)
    grad_probs = jnp.einsum(
        "qhe,khe->hqk",
        grad_heads,
        block_values.reshape(piece_rows, head_count, head_size),
        preferred_element_type=jnp.float32,
    )
    grad_scores = (probabilities * (grad_probs - products[..., None])).astype(jnp.bfloat16)
    grad_queries = score_scale * jnp.einsum(
        "hqk,khe->qhe", grad_scores, key_heads, preferred_element_type=jnp.float32
    )
    block_queries = lax.all_gather(query_flat, "ctx", axis=0, tiled=True)
    block_grads = lax.all_gather(grad_attended, "ctx", axis=0, tiled=True)
    piece_rows = block_queries.shape[0]
    query_heads = block_queries.reshape(piece_rows, head_count, head_size)
    grad_rows = block_grads.reshape(piece_rows, head_count, head_size)
    scores = (
        jnp.einsum("qhe,khe->hqk", query_heads, own_keys, preferred_element_type=jnp.float32)
        * score_scale
    )
    allowed = (all_ids[:, None] == own_ids[None, :])[None]
    probabilities = jnp.where(allowed, jnp.exp(scores - all_log[..., None]), 0.0)
    grad_values = jnp.einsum(
        "hqk,qhe->khe",
        probabilities.astype(jnp.bfloat16),
        grad_rows,
        preferred_element_type=jnp.float32,
    )
    grad_probs = jnp.einsum(
        "qhe,khe->hqk", grad_rows, own_values, preferred_element_type=jnp.float32
    )
    grad_scores = (probabilities * (grad_probs - all_products[..., None])).astype(jnp.bfloat16)
    grad_keys = score_scale * jnp.einsum(
        "hqk,qhe->khe", grad_scores, query_heads, preferred_element_type=jnp.float32
    )
    grad_keys, grad_values = (grad_keys, grad_values)
    grad_projected = jnp.concatenate(
        [
            rotary_back(grad_queries, cosines, sines).reshape(local_rows, model_width),
            rotary_back(grad_keys, cosines, sines).reshape(local_rows, model_width),
            grad_values.reshape(local_rows, model_width),
        ],
        axis=1,
    ).astype(jnp.bfloat16)
    grad_qkv = contract_rows(normed_one, grad_projected)
    grad_normed_one = contract_cols(grad_projected, qkv_back)
    _, pull_one = jax.vjp(layer_norm, source, attn_back.astype(jnp.float32))
    grad_source, grad_attn_gain = pull_one(grad_normed_one)
    grad_input = grad_middle + grad_source
    local_grads = (grad_qkv, grad_out, grad_in, grad_down, grad_attn_gain, grad_mlp_gain)
    shares = (
        lax.psum_scatter(
            local_grads[0].astype(jnp.bfloat16), "dp", scatter_dimension=0, tiled=True
        ).astype(jnp.float32),
        lax.psum_scatter(
            local_grads[1].astype(jnp.bfloat16), "dp", scatter_dimension=0, tiled=True
        ).astype(jnp.float32),
        lax.psum_scatter(
            local_grads[2].astype(jnp.bfloat16), "dp", scatter_dimension=0, tiled=True
        ).astype(jnp.float32),
        lax.psum_scatter(
            local_grads[3].astype(jnp.bfloat16), "dp", scatter_dimension=0, tiled=True
        ).astype(jnp.float32),
        lax.psum_scatter(
            local_grads[4].astype(jnp.bfloat16), "dp", scatter_dimension=0, tiled=True
        ).astype(jnp.float32),
        lax.psum_scatter(
            local_grads[5].astype(jnp.bfloat16), "dp", scatter_dimension=0, tiled=True
        ).astype(jnp.float32),
    )
    shares = (
        lax.psum(shares[0].astype(jnp.bfloat16), "ctx").astype(jnp.float32),
        lax.psum(shares[1].astype(jnp.bfloat16), "ctx").astype(jnp.float32),
        lax.psum(shares[2].astype(jnp.bfloat16), "ctx").astype(jnp.float32),
        lax.psum(shares[3].astype(jnp.bfloat16), "ctx").astype(jnp.float32),
        lax.psum(shares[4].astype(jnp.bfloat16), "ctx").astype(jnp.float32),
        lax.psum(shares[5].astype(jnp.bfloat16), "ctx").astype(jnp.float32),
    )
    return (
        result[None],
        grad_input[None],
        shares[0],
        shares[1],
        shares[2],
        shares[3],
        shares[4],
        shares[5],
    )


def solution(mesh):
    in_specs = (
        P("dp", "ctx", None),
        P("dp", "ctx"),
        P("dp", None),
        P("dp", None),
        P("dp", None),
        P("dp", None),
        P("dp"),
        P("dp"),
        P("dp", "ctx", None),
    )
    out_specs = (
        P("dp", "ctx", None),
        P("dp", "ctx", None),
        P("dp", None),
        P("dp", None),
        P("dp", None),
        P("dp", None),
        P("dp"),
        P("dp"),
    )
    return jax.shard_map(local, mesh=mesh, in_specs=in_specs, out_specs=out_specs, check_vma=False)
```

profile of v0, /device:TPU:0, one launch (start us, length us, event | category | flops | bytes accessed | tf_op | source)
XLA Modules:
  0.0 630.1 jit_solution(16062213591360769307)
XLA Ops:
  11.6 13.6 %all-reduce.7 = (bf16[768]{0:T(1024)(128)(2,1)S(1)}, bf16[768]{0:T(1024)(128)(2,1)S(1)}) all-reduce(bf16[768]{0:T(1024)(128)(2,1)S(1)} %dynamic-update-slice, bf16[768]{0:T(1024)(128)(2,1)S(1)} %dynamic-update-slice.1), channel_id=1, replica_groups=mesh['dp'=4,'ctx'=8] {'dp'}, use_global_device_ids=true, to_apply=%add | all-reduce | flops 1536 | bytes 6144
  28.5 53.9 %all-gather.10.cloned.1.call-done = bf16[768,2304]{1,0:T(8,128)(2,1)} async-done(((bf16[192,2304]{1,0:T(8,128)(2,1)}), bf16[768,2304]{1,0:T(8,128)(2,1)}) %all-gather.10.cloned.1.call-update) | async-done | bytes 3538960 | tf_op jit(solution)/shard_map/all_gather | solution.py:66
  92.2 8.7 %all-gather = s32[1,1024]{1,0:T(1,128)S(1)} all-gather(s32[1,128]{1,0:T(1,128)S(1)} %copy-done.44), channel_id=2, replica_groups=mesh['dp'=4,'ctx'=8] {'ctx'}, dimensions={1}, use_global_device_ids=true | all-gather | bytes 4608 | tf_op jit(solution)/shard_map/all_gather | solution.py:92
  101.1 12.9 %all-gather.14.cloned.1.call-done = bf16[1024,768]{1,0:T(8,128)(2,1)} async-done(((bf16[128,768]{1,0:T(8,128)(2,1)}), bf16[1024,768]{1,0:T(8,128)(2,1)}) %all-gather.14.cloned.1.call-update) | async-done | bytes 1572880 | tf_op jit(solution)/shard_map/all_gather | solution.py:90
  121.7 19.9 %all-gather.12.cloned.1.call-done = bf16[1024,768]{1,0:T(8,128)(2,1)} async-done(((bf16[128,768]{1,0:T(8,128)(2,1)}), bf16[1024,768]{1,0:T(8,128)(2,1)}) %all-gather.12.cloned.1.call-update) | async-done | bytes 1572880 | tf_op jit(solution)/shard_map/all_gather | solution.py:91
  144.2 5.8 fusion.88
  150.0 23.5 %all-gather.16.cloned.1.call-done = bf16[768,768]{1,0:T(8,128)(2,1)} async-done(((bf16[192,768]{1,0:T(8,128)(2,1)}), bf16[768,768]{1,0:T(8,128)(2,1)}) %all-gather.16.cloned.1.call-update) | async-done | bytes 1179664 | tf_op jit(solution)/shard_map/all_gather | solution.py:67
  176.0 68.1 %all-gather.18.cloned.1.call-done = bf16[768,2304]{1,0:T(8,128)(2,1)} async-done(((bf16[192,2304]{1,0:T(8,128)(2,1)}), bf16[768,2304]{1,0:T(8,128)(2,1)}) %all-gather.18.cloned.1.call-update) | async-done | bytes 3538960 | tf_op jit(solution)/shard_map/all_gather | solution.py:68
  246.8 37.7 %all-gather.20.cloned.1.call-done = bf16[1152,768]{1,0:T(8,128)(2,1)} async-done(((bf16[288,768]{1,0:T(8,128)(2,1)}), bf16[1152,768]{1,0:T(8,128)(2,1)}) %all-gather.20.cloned.1.call-update) | async-done | bytes 1769488 | tf_op jit(solution)/shard_map/all_gather | solution.py:69
  297.0 3.9 convolution_convert_fusion
  304.5 7.0 %all-gather.22.cloned.1.call-done = bf16[1024,768]{1,0:T(8,128)(2,1)} async-done(((bf16[128,768]{1,0:T(8,128)(2,1)}), bf16[1024,768]{1,0:T(8,128)(2,1)}) %all-gather.22.cloned.1.call-update) | async-done | bytes 1572880 | tf_op jit(solution)/shard_map/all_gather | solution.py:178
  314.8 10.1 %all_gather.59 = f32[12,1024]{1,0:T(8,128)} all-gather(f32[12,128]{1,0:T(8,128)S(1)} %log_add_fusion), channel_id=1, replica_groups=mesh['dp'=4,'ctx'=8] {'ctx'}, dimensions={1}, use_global_device_ids=true | all-gather | bytes 55296 | tf_op jit(solution)/shard_map/all_gather | solution.py:153
  326.0 9.1 %all_gather.61 = f32[12,1024]{1,0:T(8,128)} all-gather(f32[12,128]{1,0:T(8,128)S(1)} %bitcast.131), channel_id=1, replica_groups=mesh['dp'=4,'ctx'=8] {'ctx'}, dimensions={1}, use_global_device_ids=true | all-gather | bytes 55296 | tf_op jit(solution)/shard_map/all_gather | solution.py:154
  335.0 5.2 fusion.54
  343.0 9.0 %fusion.17 = f32[128,12,64]{0,2,1:T(8,128)} fusion(bf16[1024,12,64]{0,2,1:T(8,128)(2,1)} %bitcast.105, f32[12,1024,128]{2,1,0:T(8,128)} %fusion.54, f32[12,1024]{1,0:T(8,128)S(1)} %copy-done.30, f32[12,1024]{1,0:T(8,128)S(1)} %copy-done.28, pred[1024,128]{1,0:T(8,128)(4,1)S(1)} %copy-done.26, bf16[1024,12,64]{0,2,1:T(8,128)(2,1)} %bitcast.114, ...), kind=kOutput, calls=%fused_computation.22 | convolution fusion | flops 412090368 | bytes 10256384 | tf_op jit(solution)/shard_map/hqk,qhe->khe/dot_general | solution.py:199
  352.0 7.1 %broadcast_multiply_fusion.1 = (f32[128,12,64]{0,2,1:T(8,128)}, f32[128,12,64]{0,2,1:T(8,128)S(1)}, f32[128,12,64]{0,2,1:T(8,128)}) fusion(f32[128,64]{0,1:T(8,128)} %get-tuple-element.47, f32[128,12,64]{0,2,1:T(8,128)} %fusion.17, bf16[1024,12,64]{0,2,1:T(8,128)(2,1)S(1)} %bitcast.103, f32[12,128,1024]{2,1,0:T(8,128)} %copy-done, ...), kind=kOutput, calls=%fused_computation.102 | convolution fusion | flops 412286976 | bytes 11382784 | tf_op jit(solution)/shard_map/hqk,khe->qhe/dot_general | solution.py:175
  361.6 5.0 fusion.23
  371.4 39.2 %reduce-scatter.11.cloned.1.call-done = bf16[288,768]{1,0:T(8,128)(2,1)} async-done(((bf16[1152,768]{1,0:T(8,128)(2,1)}), bf16[288,768]{1,0:T(8,128)(2,1)}) %reduce-scatter.11.cloned.1.call-update) | async-done | bytes 442384 | tf_op jit(solution)/shard_map/reduce_scatter | solution.py:227
  410.7 67.9 %reduce-scatter.9.cloned.1.call-done = bf16[192,2304]{1,0:T(8,128)(2,1)} async-done(((bf16[768,2304]{1,0:T(8,128)(2,1)}), bf16[192,2304]{1,0:T(8,128)(2,1)}) %reduce-scatter.9.cloned.1.call-update) | async-done | bytes 884752 | tf_op jit(solution)/shard_map/reduce_scatter | solution.py:224
  478.6 69.0 %reduce-scatter.5.cloned.1.call-done = bf16[192,2304]{1,0:T(8,128)(2,1)} async-done(((bf16[768,2304]{1,0:T(8,128)(2,1)}), bf16[192,2304]{1,0:T(8,128)(2,1)}) %reduce-scatter.5.cloned.1.call-update) | async-done | bytes 884752 | tf_op jit(solution)/shard_map/reduce_scatter | solution.py:218
  548.7 3.5 fusion.47
  552.6 10.7 %all-reduce.6 = (bf16[768]{0:T(1024)(128)(2,1)S(1)}, bf16[768]{0:T(1024)(128)(2,1)S(1)}) all-reduce(bf16[768]{0:T(1024)(128)(2,1)S(1)} %get-tuple-element.10, bf16[768]{0:T(1024)(128)(2,1)S(1)} %copy-done.43), channel_id=7, replica_groups=mesh['dp'=4,'ctx'=8] {'dp'}, use_global_device_ids=true, to_apply=%region_20.21.clone | all-reduce | flops 1536 | bytes 6144
  563.5 12.1 %all-reduce.4 = (bf16[192]{0:T(256)(128)(2,1)S(1)}, bf16[192]{0:T(256)(128)(2,1)S(1)}) all-reduce(bf16[192]{0:T(256)(128)(2,1)S(1)} %dynamic-slice.3, bf16[192]{0:T(256)(128)(2,1)S(1)} %dynamic-slice.5), channel_id=1, replica_groups=mesh['dp'=4,'ctx'=8] {'ctx'}, use_global_device_ids=true, to_apply=%region_21.22 | all-reduce | flops 384 | bytes 1536 | tf_op jit(solution)/shard_map/psum | solution.py:242
  577.7 39.2 %all-reduce.10.cloned.1.call-done = (bf16[192,2304]{1,0:T(8,128)(2,1)}, bf16[192,768]{1,0:T(8,128)(2,1)}, bf16[192,2304]{1,0:T(8,128)(2,1)}, bf16[288,768]{1,0:T(8,128)(2,1)}) async-done(((bf16[192,2304]{1,0:T(8,128)(2,1)}, bf16[192,768]{1,0:T(8,128)(2,1)}, bf16[192,2304]{1,0:T(8,128)(2,1)}, bf16[288,768]{1,0:T(8,128)(2,1)}), (bf16[192,2304]{1,0:T(8,128)(2,1)}, bf16[192,768]{1,0:T(8,128)(2,1)}, ...) | async-done | bytes 2506768 | tf_op jit(solution)/shard_map/psum | solution.py:238
  (202 shorter events, 72.0 us)
Async XLA Ops:
  7.2 75.2 %all-gather.10.cloned.1.call-start = ((), (), s32[]{:S(2)}) async-start(), calls=%async_computation.4 | async-start | bytes 4423680 | tf_op jit(solution)/shard_map/all_gather | solution.py:66
  7.9 106.1 %all-gather.14.cloned.1.call-start = ((), (), s32[]{:S(2)}) async-start(), calls=%async_computation.6 | async-start | bytes 1769472 | tf_op jit(solution)/shard_map/all_gather | solution.py:90
  26.1 89.7 %copy-start.22 = (f32[128,64]{0,1:T(8,128)}, f32[128,64]{0,1:T(8,128)S(1)}, u32[]{:S(2)}) copy-start(f32[128,64]{0,1:T(8,128)S(1)} %get-tuple-element.49) | copy-start | bytes 98308
  27.3 57.9 %copy-start.34 = (f32[128]{0:T(128)}, f32[128]{0:T(128)S(1)}, u32[]{:S(2)}) copy-start(f32[128]{0:T(128)S(1)} %broadcast_multiply_fusion.6) | copy-start | bytes 1540
  28.4 56.8 %copy-start.47 = (f32[128]{0:T(128)}, f32[128]{0:T(128)S(1)}, u32[]{:S(2)}) copy-start(f32[128]{0:T(128)S(1)} %fusion.46) | copy-start | bytes 1540
  28.5 56.8 %copy-start.36 = (f32[128]{0:T(128)}, f32[128]{0:T(128)S(1)}, u32[]{:S(2)}) copy-start(f32[128]{0:T(128)S(1)} %fusion.62) | copy-start | bytes 1540
  89.6 52.1 %all-gather.12.cloned.1.call-start = ((), (), s32[]{:S(2)}) async-start(), calls=%async_computation.5 | async-start | bytes 1769472 | tf_op jit(solution)/shard_map/all_gather | solution.py:91
  90.4 83.2 %all-gather.16.cloned.1.call-start = ((), (), s32[]{:S(2)}) async-start(), calls=%async_computation.7 | async-start | bytes 1474560 | tf_op jit(solution)/shard_map/all_gather | solution.py:67
  90.9 153.2 %all-gather.18.cloned.1.call-start = ((), (), s32[]{:S(2)}) async-start(), calls=%async_computation.8 | async-start | bytes 4423680 | tf_op jit(solution)/shard_map/all_gather | solution.py:68
  91.5 192.9 %all-gather.20.cloned.1.call-start = ((), (), s32[]{:S(2)}) async-start(), calls=%async_computation.9 | async-start | bytes 2211840 | tf_op jit(solution)/shard_map/all_gather | solution.py:69
  92.1 219.4 %all-gather.22.cloned.1.call-start = ((), (), s32[]{:S(2)}) async-start(), calls=%async_computation.10 | async-start | bytes 1769472 | tf_op jit(solution)/shard_map/all_gather | solution.py:178
  101.0 43.2 %copy-start.17 = (pred[128,1024]{1,0:T(8,128)(4,1)}, pred[128,1024]{1,0:T(8,128)(4,1)S(1)}, u32[]{:S(2)}) copy-start(pred[128,1024]{1,0:T(8,128)(4,1)S(1)} %broadcast_compare_fusion.1) | copy-start | bytes 393220
  101.1 239.2 %all-gather.24.cloned.1.call-start = ((), (), s32[]{:S(2)}) async-start(), calls=%async_computation.11 | async-start | bytes 1769472 | tf_op jit(solution)/shard_map/all_gather | solution.py:179
  144.2 29.3 %copy-start.2 = (bf16[1,128,768]{2,1,0:T(8,128)(2,1)S(1)}, bf16[1,128,768]{2,1,0:T(8,128)(2,1)}, u32[]{:S(2)}) copy-start(bf16[1,128,768]{2,1,0:T(8,128)(2,1)} %param.9) | copy-start | bytes 589828
  175.2 109.2 %copy-start.14 = (bf16[1,128,768]{2,1,0:T(8,128)(2,1)S(1)}, bf16[1,128,768]{2,1,0:T(8,128)(2,1)}, u32[]{:S(2)}) copy-start(bf16[1,128,768]{2,1,0:T(8,128)(2,1)} %param.17) | copy-start | bytes 589828
  292.3 79.2 %reduce-scatter.7.cloned.1.call-start = ((), (), s32[]{:S(2)}) async-start(), calls=%async_computation.13 | async-start | bytes 1474560 | tf_op jit(solution)/shard_map/reduce_scatter | solution.py:221
  294.9 115.8 %reduce-scatter.11.cloned.1.call-start = ((), (), s32[]{:S(2)}) async-start(), calls=%async_computation.15 | async-start | bytes 2211840 | tf_op jit(solution)/shard_map/reduce_scatter | solution.py:227
  296.9 181.7 %reduce-scatter.9.cloned.1.call-start = ((), (), s32[]{:S(2)}) async-start(), calls=%async_computation.14 | async-start | bytes 4423680 | tf_op jit(solution)/shard_map/reduce_scatter | solution.py:224
  300.9 34.1 %copy-start.5 = (f32[128,768]{0,1:T(8,128)S(1)}, f32[128,768]{0,1:T(8,128)}, u32[]{:S(2)}) copy-start(f32[128,768]{0,1:T(8,128)} %copy-done.4) | copy-start | bytes 1179652
  300.9 34.1 %copy-start.7 = (f32[128,12,64]{0,2,1:T(8,128)S(1)}, f32[128,12,64]{0,2,1:T(8,128)}, u32[]{:S(2)}) copy-start(f32[128,12,64]{0,2,1:T(8,128)} %copy-done.6) | copy-start | bytes 1179652
  300.9 246.6 %reduce-scatter.5.cloned.1.call-start = ((), (), s32[]{:S(2)}) async-start(), calls=%async_computation.12 | async-start | bytes 4423680 | tf_op jit(solution)/shard_map/reduce_scatter | solution.py:218
  370.3 177.3 %copy-start.11 = (bf16[128,1152]{1,0:T(8,128)(2,1)S(1)}, bf16[128,1152]{1,0:T(8,128)(2,1)}, u32[]{:S(2)}) copy-start(bf16[128,1152]{1,0:T(8,128)(2,1)} %get-tuple-element.27) | copy-start | bytes 884740
  370.3 177.3 %copy-start.13 = (bf16[1152,768]{1,0:T(8,128)(2,1)S(1)}, bf16[1152,768]{1,0:T(8,128)(2,1)}, u32[]{:S(2)}) copy-start(bf16[1152,768]{1,0:T(8,128)(2,1)} %all-gather.20.cloned.1.call-done) | copy-start | bytes 5308420
  370.3 246.5 %all-reduce.10.cloned.1.call-start = ((), (), s32[]{:S(2)}) async-start(), calls=%async_computation.16 | async-start | bytes 5013504 | tf_op jit(solution)/shard_map/psum | solution.py:238
  (40 other events, 256.7 us)
Sparse Core Ops, SparseCore 0:
  9.6 72.7 all-gather.9
  89.7 24.2 all-gather.13
  115.9 25.6 all-gather.11
  143.0 30.4 all-gather.15
  174.9 69.0 all-gather.17
  245.5 38.8 all-gather.19
  286.9 24.5 all-gather.21
  313.4 25.8 all-gather.23
  341.6 29.1 reduce-scatter.6
  373.6 37.0 reduce-scatter.10
  413.1 65.4 reduce-scatter.8
  480.9 66.6 reduce-scatter.4
  551.7 65.0 all-reduce.9
where the time goes:
time: 631 us; the launch traced here: 630 us
  waiting for transfers between devices  441 us (70%)
  blocking collectives  64.3 us (10%)
  matrix products  62.8 us (10%)
  other arithmetic  24.1 us (4%)
  local copies, waits for them, and re-layouts  21.3 us (3%)
  between operations  16 us (3%)
    reduce_scatter x1, waiting for transfers between devices, local(): lax.psum_scatter(local_grads[0].astype(jnp.bfloat16), 'dp', scatter_dimen...  69 us
    all_gather x1, waiting for transfers between devices, local(): lax.all_gather(shards[2], 'dp', axis=0, tiled=True)  68.1 us
    reduce_scatter x1, waiting for transfers between devices, local(): lax.psum_scatter(local_grads[2].astype(jnp.bfloat16), 'dp', scatter_dimen...  67.9 us
    all_gather x1, waiting for transfers between devices, local(): lax.all_gather(shards[0], 'dp', axis=0, tiled=True)  53.9 us
    reduce_scatter x1, waiting for transfers between devices, local(): lax.psum_scatter(local_grads[3].astype(jnp.bfloat16), 'dp', scatter_dimen...  39.2 us
    psum x1, waiting for transfers between devices, local(): lax.psum(shares[0].astype(jnp.bfloat16), 'ctx').astype(jnp.float32)  39.2 us
    all_gather x1, waiting for transfers between devices, local(): lax.all_gather(shards[3], 'dp', axis=0, tiled=True)  37.7 us
    unnamed x2, blocking collectives  24.3 us
  transfers between devices with their start and end apart: 13, of which 11 were waited for; matrix products, arithmetic and copies ran while one was open for 14% of the time, Pallas kernels for 0%

commit v1 on v0

--- a/solution.py
+++ b/solution.py
@@ -7,6 +7,17 @@
 EPSILON = 1e-05
 ROPE_THETA = 160000.0
 NEGATIVE = -1e30
+
+
+def turned_line(block, name, along):
+    size = lax.axis_size(name)
+    forward = [(i, (i + 1) % size) for i in range(size)]
+    terms = [block]
+    for stride in range(1, size):
+        terms = [lax.ppermute(terms[0], name, forward), *terms]
+    out = jnp.concatenate(terms, axis=along)
+    turn = (lax.axis_index(name) + 1) * terms[-1].shape[along]
+    return jnp.roll(out, turn, axis=along)
 
 
 def layer_norm(values, gain_row):
@@ -88,7 +99,7 @@
     query_flat = queries.reshape(local_rows, model_width)
     highest = jnp.full((head_count, local_rows), NEGATIVE, jnp.float32)
     block_keys = lax.all_gather(key_flat, "ctx", axis=0, tiled=True)
-    block_values = lax.all_gather(value_flat, "ctx", axis=0, tiled=True)
+    block_values = turned_line(value_flat, "ctx", 0)
     block_ids = lax.all_gather(own_ids, "ctx", axis=0, tiled=True)
     piece_rows = block_keys.shape[0]
     scores = (

time: 631 us -> 634 us (level)
    ppermute x0 -> x7, waiting for transfers between devices: none -> 35.8 us  [turned_line(): terms = [lax.ppermute(terms[0], name, forward), *terms]]
    all_gather x1, waiting for transfers between devices: 23.5 us -> 0.01 us  [local(): lax.all_gather(shards[1], 'dp', axis=0, tiled=True)]
    all_gather x1, waiting for transfers between devices: 12.9 us -> 0.01 us  [local(): block_keys = lax.all_gather(key_flat, 'ctx', axis=0, tiled=True)]
  transfers between devices with their start and end apart: 13 -> 20, of which waited for: 11 -> 15; matrix products, arithmetic and copies ran while one was open for 14% -> 14% of each run, Pallas kernels for 0% -> 0%
where the time goes in v1:
time: 634 us; the launch traced here: 633 us
  waiting for transfers between devices  443 us (70%)
  blocking collectives  66.8 us (11%)
  matrix products  59.7 us (9%)
  other arithmetic  23.3 us (4%)
  local copies, waits for them, and re-layouts  22.1 us (3%)
  between operations  16.2 us (3%)
    reduce_scatter x1, waiting for transfers between devices, local(): lax.psum_scatter(local_grads[0].astype(jnp.bfloat16), 'dp', scatter_dimen...  69 us
    reduce_scatter x1, waiting for transfers between devices, local(): lax.psum_scatter(local_grads[2].astype(jnp.bfloat16), 'dp', scatter_dimen...  67.9 us
    all_gather x1, waiting for transfers between devices, local(): lax.all_gather(shards[2], 'dp', axis=0, tiled=True)  64.9 us
    all_gather x1, waiting for transfers between devices, local(): lax.all_gather(shards[0], 'dp', axis=0, tiled=True)  53.3 us
    psum x1, waiting for transfers between devices, local(): lax.psum(shares[0].astype(jnp.bfloat16), 'ctx').astype(jnp.float32)  39.2 us
    reduce_scatter x1, waiting for transfers between devices, local(): lax.psum_scatter(local_grads[3].astype(jnp.bfloat16), 'dp', scatter_dimen...  38.9 us
    all_gather x1, waiting for transfers between devices, local(): lax.all_gather(shards[3], 'dp', axis=0, tiled=True)  37.7 us
    ppermute x7, waiting for transfers between devices, turned_line(): terms = [lax.ppermute(terms[0], name, forward), *terms]  35.8 us
  transfers between devices with their start and end apart: 20, of which 15 were waited for; matrix products, arithmetic and copies ran while one was open for 14% of the time, Pallas kernels for 0%

profile of v1, /device:TPU:0, one launch (start us, length us, event | category | flops | bytes accessed | tf_op | source)
XLA Modules:
  0.0 632.6 jit_solution(15776542721608258040)
XLA Ops:
  11.6 13.6 %all-reduce.7 = (bf16[768]{0:T(1024)(128)(2,1)S(1)}, bf16[768]{0:T(1024)(128)(2,1)S(1)}) all-reduce(bf16[768]{0:T(1024)(128)(2,1)S(1)} %dynamic-update-slice, bf16[768]{0:T(1024)(128)(2,1)S(1)} %dynamic-update-slice.1), channel_id=1, replica_groups=mesh['dp'=4,'ctx'=8] {'dp'}, use_global_device_ids=true, to_apply=%add | all-reduce | flops 1536 | bytes 6144
  29.0 53.3 %all-gather.10.cloned.1.call-done = bf16[768,2304]{1,0:T(8,128)(2,1)} async-done(((bf16[192,2304]{1,0:T(8,128)(2,1)}), bf16[768,2304]{1,0:T(8,128)(2,1)}) %all-gather.10.cloned.1.call-update) | async-done | bytes 3538960 | tf_op jit(solution)/shard_map/all_gather | solution.py:77
  92.2 6.0 collective-permute-done
  98.2 6.0 collective-permute-done.1
  104.2 6.1 collective-permute-done.2
  110.3 6.2 collective-permute-done.3
  116.5 6.0 collective-permute-done.4
  122.5 10.9 %all-gather = s32[1,1024]{1,0:T(1,128)S(1)} all-gather(s32[1,128]{1,0:T(1,128)S(1)} %copy-done.49), channel_id=2, replica_groups=mesh['dp'=4,'ctx'=8] {'ctx'}, dimensions={1}, use_global_device_ids=true | all-gather | bytes 4608 | tf_op jit(solution)/shard_map/all_gather | solution.py:103
  134.0 5.5 collective-permute-done.6
  154.3 64.9 %all-gather.16.cloned.1.call-done = bf16[768,2304]{1,0:T(8,128)(2,1)} async-done(((bf16[192,2304]{1,0:T(8,128)(2,1)}), bf16[768,2304]{1,0:T(8,128)(2,1)}) %all-gather.16.cloned.1.call-update) | async-done | bytes 3538960 | tf_op jit(solution)/shard_map/all_gather | solution.py:79
  221.9 37.7 %all-gather.18.cloned.1.call-done = bf16[1152,768]{1,0:T(8,128)(2,1)} async-done(((bf16[288,768]{1,0:T(8,128)(2,1)}), bf16[1152,768]{1,0:T(8,128)(2,1)}) %all-gather.18.cloned.1.call-update) | async-done | bytes 1769488 | tf_op jit(solution)/shard_map/all_gather | solution.py:80
  278.0 8.4 %all-gather.22.cloned.1.call-done = bf16[1024,768]{1,0:T(8,128)(2,1)} async-done(((bf16[128,768]{1,0:T(8,128)(2,1)}), bf16[1024,768]{1,0:T(8,128)(2,1)}) %all-gather.22.cloned.1.call-update) | async-done | bytes 1572880 | tf_op jit(solution)/shard_map/all_gather | solution.py:189
  289.0 25.0 %all-gather.20.cloned.1.call-done = bf16[1024,768]{1,0:T(8,128)(2,1)} async-done(((bf16[128,768]{1,0:T(8,128)(2,1)}), bf16[1024,768]{1,0:T(8,128)(2,1)}) %all-gather.20.cloned.1.call-update) | async-done | bytes 1572880 | tf_op jit(solution)/shard_map/all_gather | solution.py:169
  317.4 10.1 %all_gather.58 = f32[12,1024]{1,0:T(8,128)} all-gather(f32[12,128]{1,0:T(8,128)S(1)} %log_add_fusion), channel_id=1, replica_groups=mesh['dp'=4,'ctx'=8] {'ctx'}, dimensions={1}, use_global_device_ids=true | all-gather | bytes 55296 | tf_op jit(solution)/shard_map/all_gather | solution.py:164
  328.5 9.4 %all_gather.60 = f32[12,1024]{1,0:T(8,128)} all-gather(f32[12,128]{1,0:T(8,128)S(1)} %bitcast.132), channel_id=1, replica_groups=mesh['dp'=4,'ctx'=8] {'ctx'}, dimensions={1}, use_global_device_ids=true | all-gather | bytes 55296 | tf_op jit(solution)/shard_map/all_gather | solution.py:165
  337.9 5.2 fusion.54
  345.8 9.0 %fusion.17 = f32[128,12,64]{0,2,1:T(8,128)} fusion(bf16[1024,12,64]{0,2,1:T(8,128)(2,1)} %bitcast.106, f32[12,1024,128]{2,1,0:T(8,128)} %fusion.54, f32[12,1024]{1,0:T(8,128)S(1)} %copy-done.34, f32[12,1024]{1,0:T(8,128)S(1)} %copy-done.32, pred[1024,128]{1,0:T(8,128)(4,1)S(1)} %copy-done.30, bf16[1024,12,64]{0,2,1:T(8,128)(2,1)} %bitcast.113, ...), kind=kOutput, calls=%fused_computation.22 | convolution fusion | flops 412090368 | bytes 10256384 | tf_op jit(solution)/shard_map/hqk,qhe->khe/dot_general | solution.py:210
  354.8 7.1 %broadcast_multiply_fusion.1 = (f32[128,12,64]{0,2,1:T(8,128)}, f32[128,12,64]{0,2,1:T(8,128)S(1)}, f32[128,12,64]{0,2,1:T(8,128)}) fusion(f32[128,64]{0,1:T(8,128)} %get-tuple-element.47, f32[128,12,64]{0,2,1:T(8,128)} %fusion.17, bf16[1024,12,64]{0,2,1:T(8,128)(2,1)S(1)} %bitcast.104, f32[12,128,1024]{2,1,0:T(8,128)} %copy-done, ...), kind=kOutput, calls=%fused_computation.102 | convolution fusion | flops 412286976 | bytes 11382784 | tf_op jit(solution)/shard_map/hqk,khe->qhe/dot_general | solution.py:186
  374.3 38.9 %reduce-scatter.11.cloned.1.call-done = bf16[288,768]{1,0:T(8,128)(2,1)} async-done(((bf16[1152,768]{1,0:T(8,128)(2,1)}), bf16[288,768]{1,0:T(8,128)(2,1)}) %reduce-scatter.11.cloned.1.call-update) | async-done | bytes 442384 | tf_op jit(solution)/shard_map/reduce_scatter | solution.py:238
  413.2 67.9 %reduce-scatter.9.cloned.1.call-done = bf16[192,2304]{1,0:T(8,128)(2,1)} async-done(((bf16[768,2304]{1,0:T(8,128)(2,1)}), bf16[192,2304]{1,0:T(8,128)(2,1)}) %reduce-scatter.9.cloned.1.call-update) | async-done | bytes 884752 | tf_op jit(solution)/shard_map/reduce_scatter | solution.py:235
  481.2 69.0 %reduce-scatter.5.cloned.1.call-done = bf16[192,2304]{1,0:T(8,128)(2,1)} async-done(((bf16[768,2304]{1,0:T(8,128)(2,1)}), bf16[192,2304]{1,0:T(8,128)(2,1)}) %reduce-scatter.5.cloned.1.call-update) | async-done | bytes 884752 | tf_op jit(solution)/shard_map/reduce_scatter | solution.py:229
  555.1 10.8 %all-reduce.6 = (bf16[768]{0:T(1024)(128)(2,1)S(1)}, bf16[768]{0:T(1024)(128)(2,1)S(1)}) all-reduce(bf16[768]{0:T(1024)(128)(2,1)S(1)} %get-tuple-element.10, bf16[768]{0:T(1024)(128)(2,1)S(1)} %copy-done.48), channel_id=7, replica_groups=mesh['dp'=4,'ctx'=8] {'dp'}, use_global_device_ids=true, to_apply=%region_20.21.clone | all-reduce | flops 1536 | bytes 6144
  566.0 12.1 %all-reduce.4 = (bf16[192]{0:T(256)(128)(2,1)S(1)}, bf16[192]{0:T(256)(128)(2,1)S(1)}) all-reduce(bf16[192]{0:T(256)(128)(2,1)S(1)} %dynamic-slice.3, bf16[192]{0:T(256)(128)(2,1)S(1)} %dynamic-slice.5), channel_id=1, replica_groups=mesh['dp'=4,'ctx'=8] {'ctx'}, use_global_device_ids=true, to_apply=%region_21.22 | all-reduce | flops 384 | bytes 1536 | tf_op jit(solution)/shard_map/psum | solution.py:253
  580.2 39.2 %all-reduce.10.cloned.1.call-done = (bf16[192,2304]{1,0:T(8,128)(2,1)}, bf16[192,768]{1,0:T(8,128)(2,1)}, bf16[192,2304]{1,0:T(8,128)(2,1)}, bf16[288,768]{1,0:T(8,128)(2,1)}) async-done(((bf16[192,2304]{1,0:T(8,128)(2,1)}, bf16[192,768]{1,0:T(8,128)(2,1)}, bf16[192,2304]{1,0:T(8,128)(2,1)}, bf16[288,768]{1,0:T(8,128)(2,1)}), (bf16[192,2304]{1,0:T(8,128)(2,1)}, bf16[192,768]{1,0:T(8,128)(2,1)}, ...) | async-done | bytes 2506768 | tf_op jit(solution)/shard_map/psum | solution.py:249
  (246 shorter events, 88.3 us)
Async XLA Ops:
  7.2 75.2 %all-gather.10.cloned.1.call-start = ((), (), s32[]{:S(2)}) async-start(), calls=%async_computation.4 | async-start | bytes 4423680 | tf_op jit(solution)/shard_map/all_gather | solution.py:77
  7.9 135.6 %all-gather.12.cloned.1.call-start = ((), (), s32[]{:S(2)}) async-start(), calls=%async_computation.5 | async-start | bytes 1769472 | tf_op jit(solution)/shard_map/all_gather | solution.py:101
  89.6 62.2 %all-gather.14.cloned.1.call-start = ((), (), s32[]{:S(2)}) async-start(), calls=%async_computation.6 | async-start | bytes 1474560 | tf_op jit(solution)/shard_map/all_gather | solution.py:78
  90.3 128.9 %all-gather.16.cloned.1.call-start = ((), (), s32[]{:S(2)}) async-start(), calls=%async_computation.7 | async-start | bytes 4423680 | tf_op jit(solution)/shard_map/all_gather | solution.py:79
  90.9 168.6 %all-gather.18.cloned.1.call-start = ((), (), s32[]{:S(2)}) async-start(), calls=%async_computation.8 | async-start | bytes 2211840 | tf_op jit(solution)/shard_map/all_gather | solution.py:80
  91.5 195.0 %all-gather.22.cloned.1.call-start = ((), (), s32[]{:S(2)}) async-start(), calls=%async_computation.10 | async-start | bytes 1769472 | tf_op jit(solution)/shard_map/all_gather | solution.py:189
  92.1 222.0 %all-gather.20.cloned.1.call-start = ((), (), s32[]{:S(2)}) async-start(), calls=%async_computation.9 | async-start | bytes 1769472 | tf_op jit(solution)/shard_map/all_gather | solution.py:169
  92.2 6.0 collective-permute-start
  98.2 6.0 collective-permute-start.1
  104.2 6.1 collective-permute-start.2
  110.3 6.2 collective-permute-start.3
  116.5 6.0 collective-permute-start.4
  122.5 10.9 %collective-permute-start.5 = (bf16[128,768]{1,0:T(8,128)(2,1)S(1)}, bf16[128,768]{1,0:T(8,128)(2,1)S(1)}, u32[]{:S(2)}, u32[]{:S(2)}) collective-permute-start(bf16[128,768]{1,0:T(8,128)(2,1)S(1)} %collective-permute-done.4), channel_id=1, source_target_pairs={{0,1},{1,2},{2,3},{3,4},{4,5},{5,6},{6,7},{7,0},{8,9},{9,10},{10,1... | collective-permute-start | bytes 589832 | tf_op jit(solution)/shard_map/ppermute | solution.py:17
  133.4 6.1 collective-permute-start.6
  133.8 209.3 %all-gather.24.cloned.1.call-start = ((), (), s32[]{:S(2)}) async-start(), calls=%async_computation.11 | async-start | bytes 1769472 | tf_op jit(solution)/shard_map/all_gather | solution.py:190
  153.6 106.0 %copy-start.16 = (bf16[1,128,768]{2,1,0:T(8,128)(2,1)S(1)}, bf16[1,128,768]{2,1,0:T(8,128)(2,1)}, u32[]{:S(2)}) copy-start(bf16[1,128,768]{2,1,0:T(8,128)(2,1)} %param.17) | copy-start | bytes 589828
  267.3 107.0 %reduce-scatter.7.cloned.1.call-start = ((), (), s32[]{:S(2)}) async-start(), calls=%async_computation.13 | async-start | bytes 1474560 | tf_op jit(solution)/shard_map/reduce_scatter | solution.py:232
  269.8 143.4 %reduce-scatter.11.cloned.1.call-start = ((), (), s32[]{:S(2)}) async-start(), calls=%async_computation.15 | async-start | bytes 2211840 | tf_op jit(solution)/shard_map/reduce_scatter | solution.py:238
  271.8 209.3 %reduce-scatter.9.cloned.1.call-start = ((), (), s32[]{:S(2)}) async-start(), calls=%async_computation.14 | async-start | bytes 4423680 | tf_op jit(solution)/shard_map/reduce_scatter | solution.py:235
  275.9 274.2 %reduce-scatter.5.cloned.1.call-start = ((), (), s32[]{:S(2)}) async-start(), calls=%async_computation.12 | async-start | bytes 4423680 | tf_op jit(solution)/shard_map/reduce_scatter | solution.py:229
  278.0 59.9 %copy-start.5 = (f32[128,768]{0,1:T(8,128)S(1)}, f32[128,768]{0,1:T(8,128)}, u32[]{:S(2)}) copy-start(f32[128,768]{0,1:T(8,128)} %copy-done.4) | copy-start | bytes 1179652
  373.1 177.0 %copy-start.11 = (bf16[128,1152]{1,0:T(8,128)(2,1)S(1)}, bf16[128,1152]{1,0:T(8,128)(2,1)}, u32[]{:S(2)}) copy-start(bf16[128,1152]{1,0:T(8,128)(2,1)} %get-tuple-element.27) | copy-start | bytes 884740
  373.1 177.0 %copy-start.15 = (bf16[1152,768]{1,0:T(8,128)(2,1)S(1)}, bf16[1152,768]{1,0:T(8,128)(2,1)}, u32[]{:S(2)}) copy-start(bf16[1152,768]{1,0:T(8,128)(2,1)} %all-gather.18.cloned.1.call-done) | copy-start | bytes 5308420
  373.1 246.3 %all-reduce.10.cloned.1.call-start = ((), (), s32[]{:S(2)}) async-start(), calls=%async_computation.16 | async-start | bytes 5013504 | tf_op jit(solution)/shard_map/psum | solution.py:249
  (53 other events, 535.7 us)
Sparse Core Ops, SparseCore 0:
  9.6 72.7 all-gather.9
  89.7 26.4 all-gather.11
  117.8 30.7 all-gather.13
  150.0 69.0 all-gather.15
  220.6 38.8 all-gather.17
  261.8 24.5 all-gather.21
  288.3 25.6 all-gather.19
  315.9 25.8 all-gather.23
  344.1 29.1 reduce-scatter.6
  376.1 37.0 reduce-scatter.10
  415.7 65.4 reduce-scatter.8
  483.4 66.6 reduce-scatter.4
  554.3 65.0 all-reduce.9
